TPU v7x, 512 devices: a whole 4x4x16 slice. The times are simulated.
512 devices in a mesh: blk: 256 (over z, x, y_hi, core), head: 2 (over y_lo).
Axes of the slice: x: 4, y: 4 (y_hi: 2, y_lo: 2; y = y_hi * 2 + y_lo), z: 16, core: 2. Of those that a mesh axis runs over, the one named last changes fastest.
Arguments:
- ref_a: bfloat16 [32768, 1024], P('blk', 'head'), may hold values from -8 to 8
- val_a: bfloat16 [32768, 1024], P('blk', 'head'), may hold values from -6 to 6
- ref_b: bfloat16 [32768, 1024], P('blk', 'head'), may hold values from -8 to 8
- val_b: bfloat16 [32768, 1024], P('blk', 'head'), may hold values from -6 to 6
- w_out_a: bfloat16 [1024, 1024], P('head'), may hold values from -0.1875 to 0.1875
- w_out_b: bfloat16 [1024, 1024], P('head'), may hold values from -0.1875 to 0.1875
Outputs:
- out_a: bfloat16 [32768, 1024], P(('blk', 'head'))
- out_b: bfloat16 [32768, 1024], P(('blk', 'head'))
All inputs are finite; a program needn't handle non-finite values.
Results may differ from a plain program's by a relative error of at most 0.0055.
Values may be sent and summed in bfloat16 or wider, within the bound.
A program may use at most 64 MiB of HBM per device.

v0:
```python
import functools
import math

import jax
import jax.numpy as jnp
from jax import lax
from jax.experimental import pallas as pl
from jax.experimental.pallas import tpu as pltpu
from jax.sharding import PartitionSpec as P


ROWS = 128
HALF = 64
PAIR = 128
WIDTH = 1024
CHUNKS = 2
PIECE = WIDTH // CHUNKS
SCORE = 0.125 * math.log2(math.e)
BF16 = jnp.bfloat16
F32 = jnp.float32


def attend(query, keys, values):
    lane = lax.broadcasted_iota(jnp.int32, (ROWS, PAIR), 1)
    query = query.astype(F32)
    zero = jnp.zeros_like(query)
    both = jnp.concatenate(
        [jnp.where(lane < HALF, query, zero), jnp.where(lane < HALF, zero, query)], axis=0
    ).astype(BF16)
    parts = []
    for key, value in zip(keys, values):
        scores = lax.dot_general(key, both, (((1,), (1,)), ((), ())), preferred_element_type=F32)
        top = jnp.max(scores, axis=0, keepdims=True)
        expo = jnp.exp2((scores - top) * SCORE)
        accum = jnp.dot(value, expo.astype(BF16), preferred_element_type=F32)
        parts.append((top, jnp.sum(expo, axis=0, keepdims=True), accum[:HALF, :ROWS], accum[HALF:, ROWS:]))
    top = functools.reduce(jnp.maximum, [part[0] for part in parts])
    scales = [jnp.exp2((part[0] - top) * SCORE) for part in parts]
    total = sum(scale * part[1] for scale, part in zip(scales, parts))
    first = sum(scale[:, :ROWS] * part[2] for scale, part in zip(scales, parts))
    second = sum(scale[:, ROWS:] * part[3] for scale, part in zip(scales, parts))
    result = jnp.concatenate([first / total[:, :ROWS], second / total[:, ROWS:]], axis=0)
    return result.T.astype(BF16)


def kernel(
    count,
    ref_a,
    val_a,
    ref_b,
    val_b,
    w_a,
    w_b,
    out_a,
    out_b,
    staged,
    held,
    turned,
    weights,
    attn,
    gathered,
    outgoing,
    incoming,
    own,
    weight_sem,
    stage_sem,
    share_send,
    share_recv,
    band_send,
    band_recv,
    attn_send,
    attn_recv,
    part_send,
    part_recv,
):
    blk, head = lax.axis_index("blk"), lax.axis_index("head")
    place = lax.rem(blk, 4)
    base = blk - place
    other = 1 - head
    following = lax.rem(blk + 4, count)
    previous = lax.rem(blk + count - 4, count)
    swapped = lax.rem(place, 2) * 2 + place // 2

    barrier = pltpu.get_barrier_semaphore()
    for p in range(4):
        pl.semaphore_signal(barrier, inc=1, device_id={"blk": base + p, "head": other})
    pl.semaphore_signal(barrier, inc=1, device_id={"blk": following})
    pl.semaphore_signal(barrier, inc=1, device_id={"blk": previous})

    loads = [
        pltpu.make_async_copy(w, weights.at[side], weight_sem.at[side])
        for side, w in enumerate((w_a, w_b))
    ]
    for side, pair in enumerate(((ref_a, val_a), (ref_b, val_b))):
        for p in range(4):
            for t in range(2):
                pltpu.make_async_copy(
                    pair[t].at[:, pl.ds(p * PAIR, PAIR)], staged.at[side, p, t], stage_sem.at[side]
                ).start()
    for load in loads:
        load.start()

    pl.semaphore_wait(barrier, 6)

    def landed(ref, sem):
        pltpu.make_async_remote_copy(
            src_ref=ref, dst_ref=ref, send_sem=sem, recv_sem=sem, device_id={"head": other}
        ).wait_recv()

    def left(ref, sem):
        pltpu.make_async_remote_copy(
            src_ref=ref, dst_ref=ref, send_sem=sem, recv_sem=sem, device_id={"head": other}
        ).wait_send()

    def share(side, p):
        return pltpu.make_async_remote_copy(
            src_ref=staged.at[side, p],
            dst_ref=held.at[side, place + 1 + side],
            send_sem=share_send.at[side],
            recv_sem=share_recv.at[side, place],
            device_id={"blk": base + p, "head": other},
        )

    ahead = place // 2
    pltpu.make_async_copy(staged.at[ahead], staged.at[ahead], stage_sem.at[ahead]).wait()
    for p in range(4):
        share(ahead, p).start()
    behind = 1 - ahead
    pltpu.make_async_copy(staged.at[behind], staged.at[behind], stage_sem.at[behind]).wait()
    left(staged.at[ahead], share_send.at[ahead])
    for p in range(4):
        share(behind, p).start()

    def wait_share(side, blocks):
        for block in blocks:
            landed(held.at[side, block + 1 + side], share_recv.at[side, block])

    bands = ((1, 4, 0, 2, True), (0, 1, 5, 2, False), (0, 4, 0, 1, True), (1, 2, 6, 1, False))

    def band(index):
        side, first, target, blocks, forward = bands[index]
        return pltpu.make_async_remote_copy(
            src_ref=held.at[side, pl.ds(first, blocks)],
            dst_ref=held.at[side, pl.ds(target, blocks)],
            send_sem=band_send,
            recv_sem=band_recv.at[index],
            device_id={"blk": following if forward else previous},
        )

    def turn(side, first, blocks):
        for position in range(first, first + blocks):
            turned[side, position] = held[side, position, 1].T

    def attn_copies(side, n):
        if n in (0, 3):
            pieces = ((n, pl.ds(0, ROWS)),)
        else:
            pieces = (
                (n, pl.ds(pl.multiple_of(other * HALF, HALF), HALF)),
                (3 - n, pl.ds(pl.multiple_of(head * HALF, HALF), HALF)),
            )
        return [
            pltpu.make_async_remote_copy(
                src_ref=attn.at[side, n, rows],
                dst_ref=gathered.at[side, place, rows],
                send_sem=attn_send.at[side],
                recv_sem=attn_recv.at[side],
                device_id={"blk": base + target, "head": other},
            )
            for target, rows in pieces
        ]

    def work(*tasks):
        for side, n in tasks:
            keys = [held[1 - side, n + k, 0] for k in range(4)]
            values = [turned[1 - side, n + k] for k in range(4)]
            attn[side, n] = attend(held[side, n + 1 + side, 0], keys, values)
        for side, n in tasks:
            for copy in attn_copies(side, n):
                copy.start()

    for index, (side, first, _, blocks, _) in enumerate(bands):
        wait_share(side, range(first - 1 - side, first - 1 - side + blocks))
        band(index).start()
    wait_share(0, (2,))
    wait_share(1, (1,))
    turn(0, 1, 4)
    turn(1, 2, 4)
    work((0, 2), (1, 1))
    band(1).wait_recv()
    band(3).wait_recv()
    turn(0, 5, 2)
    turn(1, 6, 1)
    work((0, 3), (1, 2), (1, 3))
    band(0).wait_recv()
    turn(1, 0, 2)
    work((0, 1), (0, 0))
    band(2).wait_recv()
    turn(0, 0, 1)
    work((1, 0),)

    mine = pl.ds(pl.multiple_of(head * HALF, HALF), HALF)
    theirs = pl.ds(pl.multiple_of(other * HALF, HALF), HALF)

    def part(side, chunk):
        return pltpu.make_async_remote_copy(
            src_ref=outgoing.at[side, chunk],
            dst_ref=incoming.at[side, chunk],
            send_sem=part_send.at[side],
            recv_sem=part_recv.at[side, chunk],
            device_id={"blk": base + swapped, "head": other},
        )

    for side in range(2):
        loads[side].wait()
        landed(gathered.at[side], attn_recv.at[side])
        rows = jnp.concatenate(
            [
                jnp.concatenate([gathered[side, p, half] for p in range(4)], axis=1)
                for half in (mine, theirs)
            ],
            axis=0,
        )
        for chunk in range(CHUNKS):
            product = jnp.dot(
                rows,
                weights[side, :, chunk * PIECE : (chunk + 1) * PIECE],
                preferred_element_type=F32,
            )
            outgoing[side, chunk] = product[HALF:].astype(BF16)
            part(side, chunk).start()
            own[side, chunk] = product[:HALF]

    left(staged.at[behind], share_send.at[behind])
    left(held.at[0, pl.ds(0, 6)], band_send)
    for side in range(2):
        left(attn.at[side], attn_send.at[side])
        left(outgoing.at[side], part_send.at[side])

    for side, out in enumerate((out_a, out_b)):
        for chunk in range(CHUNKS):
            part(side, chunk).wait_recv()
            out[:, chunk * PIECE : (chunk + 1) * PIECE] = (
                own[side, chunk] + incoming[side, chunk].astype(F32)
            ).astype(BF16)


def solution(mesh):
    count = mesh.shape["blk"]

    def shards(ref_a, val_a, ref_b, val_b, w_out_a, w_out_b):
        hbm = pl.BlockSpec(memory_space=pltpu.HBM)
        vmem = pl.BlockSpec(memory_space=pltpu.VMEM)
        out = pltpu.VMEM((HALF, WIDTH), BF16)
        return pl.pallas_call(
            functools.partial(kernel, count),
            out_shape=(out, out),
            in_specs=[hbm] * 6,
            out_specs=(vmem, vmem),
            scratch_shapes=[
                pltpu.VMEM((2, 4, 2, ROWS, PAIR), BF16),
                pltpu.VMEM((2, 7, 2, ROWS, PAIR), BF16),
                pltpu.VMEM((2, 7, PAIR, ROWS), BF16),
                pltpu.VMEM((2, WIDTH // 2, WIDTH), BF16),
                pltpu.VMEM((2, 4, ROWS, PAIR), BF16),
                pltpu.VMEM((2, 4, ROWS, PAIR), BF16),
                pltpu.VMEM((2, CHUNKS, HALF, PIECE), BF16),
                pltpu.VMEM((2, CHUNKS, HALF, PIECE), BF16),
                pltpu.VMEM((2, CHUNKS, HALF, PIECE), F32),
                pltpu.SemaphoreType.DMA((2,)),
                pltpu.SemaphoreType.DMA((2,)),
                pltpu.SemaphoreType.DMA((2,)),
                pltpu.SemaphoreType.DMA((2, 4)),
                pltpu.SemaphoreType.DMA,
                pltpu.SemaphoreType.DMA((4,)),
                pltpu.SemaphoreType.DMA((2,)),
                pltpu.SemaphoreType.DMA((2,)),
                pltpu.SemaphoreType.DMA((2,)),
                pltpu.SemaphoreType.DMA((2, CHUNKS)),
            ],
            compiler_params=pltpu.CompilerParams(
                collective_id=0, has_side_effects=True, vmem_limit_bytes=32 * 1024 * 1024
            ),
        )(
            *(
                pltpu.with_memory_space_constraint(array, pltpu.HBM)
                for array in (ref_a, val_a, ref_b, val_b, w_out_a, w_out_b)
            )
        )

    return jax.shard_map(
        shards,
        mesh=mesh,
        in_specs=(
            P("blk", "head"),
            P("blk", "head"),
            P("blk", "head"),
            P("blk", "head"),
            P("head", None),
            P("head", None),
        ),
        out_specs=(P(("blk", "head"), None), P(("blk", "head"), None)),
        check_vma=False,
    )
```

profile of v0, /device:TPU:1, one launch (start us, length us, event | category | flops | bytes accessed | tf_op | source)
XLA Modules:
  0.0 37.3 jit_solution(7400672492505386546)
XLA Ops:
  0.6 35.4 %shard_map.77 = (bf16[64,1024]{1,0:T(8,128)(2,1)S(1)}, bf16[64,1024]{1,0:T(8,128)(2,1)S(1)}) custom-call(bf16[128,512]{1,0:T(8,128)(2,1)} %ref_a.1, bf16[128,512]{1,0:T(8,128)(2,1)} %val_a.1, bf16[128,512]{1,0:T(8,128)(2,1)} %ref_b.1, bf16[128,512]{1,0:T(8,128)(2,1)} %val_b.1, bf16[512,1024]{1,0:T(8,128)(2,1)} %w_a.1, bf16[512,1024]{1,0:T(8,128)(2,1)} %w_b.1), custom_call_target="tpu_custom_call" | custom-call | tf_op jit(solution)/shard_map/pallas_call | solution.py:255
  36.0 0.7 %copy.10 = bf16[64,1024]{1,0:T(8,128)(2,1)} copy(bf16[64,1024]{1,0:T(8,128)(2,1)S(1)} %get-tuple-element.2) | data formatting | bytes 262144
  36.7 0.7 %copy.11 = bf16[64,1024]{1,0:T(8,128)(2,1)} copy(bf16[64,1024]{1,0:T(8,128)(2,1)S(1)} %get-tuple-element.3) | data formatting | bytes 262144
where the time goes:
time: 37.5 us; the launch traced here: 37.3 us
  Pallas kernels  35.4 us (94%)
  local copies, waits for them, and re-layouts  1.31 us (3%)
  between operations  0.64 us (2%)
    pallas_call x1, Pallas kernels, shards(): pl.pallas_call(functools.partial(kernel, count), out_shape=(out, out), in...  35.4 us
    unnamed x2, local copies, waits for them, and re-layouts  1.31 us

commit v1 on v0

--- a/solution.py
+++ b/solution.py
@@ -20,25 +20,36 @@
 F32 = jnp.float32
 
 
-def attend(query, keys, values):
+def split_heads(query):
     lane = lax.broadcasted_iota(jnp.int32, (ROWS, PAIR), 1)
     query = query.astype(F32)
     zero = jnp.zeros_like(query)
-    both = jnp.concatenate(
+    return jnp.concatenate(
         [jnp.where(lane < HALF, query, zero), jnp.where(lane < HALF, zero, query)], axis=0
     ).astype(BF16)
-    parts = []
-    for key, value in zip(keys, values):
-        scores = lax.dot_general(key, both, (((1,), (1,)), ((), ())), preferred_element_type=F32)
-        top = jnp.max(scores, axis=0, keepdims=True)
-        expo = jnp.exp2((scores - top) * SCORE)
-        accum = jnp.dot(value, expo.astype(BF16), preferred_element_type=F32)
-        parts.append((top, jnp.sum(expo, axis=0, keepdims=True), accum[:HALF, :ROWS], accum[HALF:, ROWS:]))
+
+
+def pair_part(both, key, value):
+    scores = lax.dot_general(key, both, (((1,), (1,)), ((), ())), preferred_element_type=F32)
+    top = jnp.max(scores, axis=0, keepdims=True)
+    expo = jnp.exp2((scores - top) * SCORE)
+    accum = jnp.dot(value, expo.astype(BF16), preferred_element_type=F32)
+    return top, jnp.sum(expo, axis=0, keepdims=True), accum[:HALF, :ROWS], accum[HALF:, ROWS:]
+
+
+def merge_parts(parts):
     top = functools.reduce(jnp.maximum, [part[0] for part in parts])
     scales = [jnp.exp2((part[0] - top) * SCORE) for part in parts]
-    total = sum(scale * part[1] for scale, part in zip(scales, parts))
-    first = sum(scale[:, :ROWS] * part[2] for scale, part in zip(scales, parts))
-    second = sum(scale[:, ROWS:] * part[3] for scale, part in zip(scales, parts))
+    return (
+        top,
+        sum(scale * part[1] for scale, part in zip(scales, parts)),
+        sum(scale[:, :ROWS] * part[2] for scale, part in zip(scales, parts)),
+        sum(scale[:, ROWS:] * part[3] for scale, part in zip(scales, parts)),
+    )
+
+
+def finish(part):
+    _, total, first, second = part
     result = jnp.concatenate([first / total[:, :ROWS], second / total[:, ROWS:]], axis=0)
     return result.T.astype(BF16)
 
@@ -51,12 +62,13 @@
     val_b,
     w_a,
     w_b,
-    out_a,
-    out_b,
+    out,
     staged,
     held,
     turned,
     weights,
+    stats,
+    sums,
     attn,
     gathered,
     outgoing,
@@ -127,7 +139,11 @@
         share(ahead, p).start()
     behind = 1 - ahead
     pltpu.make_async_copy(staged.at[behind], staged.at[behind], stage_sem.at[behind]).wait()
-    left(staged.at[ahead], share_send.at[ahead])
+
+    @pl.when((place == 1) | (place == 2))
+    def _():
+        left(staged.at[ahead], share_send.at[ahead])
+
     for p in range(4):
         share(behind, p).start()
 
@@ -170,11 +186,34 @@
             for target, rows in pieces
         ]
 
-    def work(*tasks):
-        for side, n in tasks:
-            keys = [held[1 - side, n + k, 0] for k in range(4)]
-            values = [turned[1 - side, n + k] for k in range(4)]
-            attn[side, n] = attend(held[side, n + 1 + side, 0], keys, values)
+    def pairs(side, n, positions):
+        both = split_heads(held[side, n + 1 + side, 0])
+        return [
+            pair_part(both, held[1 - side, position, 0], turned[1 - side, position])
+            for position in positions
+        ]
+
+    def ready(side, n, part):
+        attn[side, n] = finish(part)
+
+    def begin(side, n, positions):
+        part = merge_parts(pairs(side, n, positions))
+        if len(positions) == 4:
+            ready(side, n, part)
+        else:
+            stats[side, n, 0:1], stats[side, n, 1:2] = part[0], part[1]
+            sums[side, n, :HALF], sums[side, n, HALF:] = part[2], part[3]
+
+    def complete(side, n, positions):
+        state = (
+            stats[side, n, 0:1],
+            stats[side, n, 1:2],
+            sums[side, n, :HALF],
+            sums[side, n, HALF:],
+        )
+        ready(side, n, merge_parts([state] + pairs(side, n, positions)))
+
+    def give(*tasks):
         for side, n in tasks:
             for copy in attn_copies(side, n):
                 copy.start()
@@ -186,18 +225,32 @@
     wait_share(1, (1,))
     turn(0, 1, 4)
     turn(1, 2, 4)
-    work((0, 2), (1, 1))
+    begin(0, 2, (2, 3, 4, 5))
+    begin(1, 1, (1, 2, 3, 4))
+    give((0, 2), (1, 1))
+    begin(0, 3, (3, 4, 5))
+    begin(1, 2, (2, 3, 4))
+    begin(1, 3, (3, 4))
+    begin(0, 1, (2, 3, 4))
+    begin(0, 0, (2, 3))
+    begin(1, 0, (1, 2, 3))
     band(1).wait_recv()
     band(3).wait_recv()
     turn(0, 5, 2)
     turn(1, 6, 1)
-    work((0, 3), (1, 2), (1, 3))
+    complete(0, 3, (6,))
+    complete(1, 2, (5,))
+    complete(1, 3, (5, 6))
+    give((0, 3), (1, 2), (1, 3))
     band(0).wait_recv()
     turn(1, 0, 2)
-    work((0, 1), (0, 0))
+    complete(0, 1, (1,))
+    complete(0, 0, (0, 1))
+    give((0, 1), (0, 0))
     band(2).wait_recv()
     turn(0, 0, 1)
-    work((1, 0),)
+    complete(1, 0, (0,))
+    give((1, 0),)
 
     mine = pl.ds(pl.multiple_of(head * HALF, HALF), HALF)
     theirs = pl.ds(pl.multiple_of(other * HALF, HALF), HALF)
@@ -231,16 +284,20 @@
             part(side, chunk).start()
             own[side, chunk] = product[:HALF]
 
+    @pl.when((place == 0) | (place == 3))
+    def _():
+        left(staged.at[ahead], share_send.at[ahead])
+
     left(staged.at[behind], share_send.at[behind])
     left(held.at[0, pl.ds(0, 6)], band_send)
     for side in range(2):
         left(attn.at[side], attn_send.at[side])
         left(outgoing.at[side], part_send.at[side])
 
-    for side, out in enumerate((out_a, out_b)):
+    for side in range(2):
         for chunk in range(CHUNKS):
             part(side, chunk).wait_recv()
-            out[:, chunk * PIECE : (chunk + 1) * PIECE] = (
+            out[side, :, chunk * PIECE : (chunk + 1) * PIECE] = (
                 own[side, chunk] + incoming[side, chunk].astype(F32)
             ).astype(BF16)
 
@@ -251,17 +308,19 @@
     def shards(ref_a, val_a, ref_b, val_b, w_out_a, w_out_b):
         hbm = pl.BlockSpec(memory_space=pltpu.HBM)
         vmem = pl.BlockSpec(memory_space=pltpu.VMEM)
-        out = pltpu.VMEM((HALF, WIDTH), BF16)
-        return pl.pallas_call(
+        out = pltpu.VMEM((2, HALF, WIDTH), BF16)
+        results = pl.pallas_call(
             functools.partial(kernel, count),
-            out_shape=(out, out),
+            out_shape=out,
             in_specs=[hbm] * 6,
-            out_specs=(vmem, vmem),
+            out_specs=vmem,
             scratch_shapes=[
                 pltpu.VMEM((2, 4, 2, ROWS, PAIR), BF16),
                 pltpu.VMEM((2, 7, 2, ROWS, PAIR), BF16),
                 pltpu.VMEM((2, 7, PAIR, ROWS), BF16),
                 pltpu.VMEM((2, WIDTH // 2, WIDTH), BF16),
+                pltpu.VMEM((2, 4, 8, 2 * ROWS), F32),
+                pltpu.VMEM((2, 4, PAIR, ROWS), F32),
                 pltpu.VMEM((2, 4, ROWS, PAIR), BF16),
                 pltpu.VMEM((2, 4, ROWS, PAIR), BF16),
                 pltpu.VMEM((2, CHUNKS, HALF, PIECE), BF16),
@@ -287,6 +346,7 @@
                 for array in (ref_a, val_a, ref_b, val_b, w_out_a, w_out_b)
             )
         )
+        return results[0], results[1]
 
     return jax.shard_map(
         shards,

time: 37.5 us -> 38 us (1.013)
  Pallas kernels: 35.4 us -> 36.5 us
  local copies, waits for them, and re-layouts: 1.31 us -> 0.72 us
    unnamed x2 -> x0, local copies, waits for them, and re-layouts: 1.31 us -> none
    pallas_call x1, Pallas kernels: 35.4 us -> 36.5 us  [shards(): pl.pallas_call(functools.partial(kernel, count), out_shape=out, in_specs=...]
    squeeze x0 -> x1, local copies, waits for them, and re-layouts: none -> 0.72 us  [shards(): return (results[0], results[1])]
where the time goes in v1:
time: 38 us; the launch traced here: 37.9 us
  Pallas kernels  36.5 us (96%)
  local copies, waits for them, and re-layouts  0.72 us (2%)
  between operations  0.64 us (2%)
    pallas_call x1, Pallas kernels, shards(): pl.pallas_call(functools.partial(kernel, count), out_shape=out, in_specs=...  36.5 us

profile of v1, /device:TPU:1, one launch (start us, length us, event | category | flops | bytes accessed | tf_op | source)
XLA Modules:
  0.0 37.9 jit_solution(17528777296089114186)
XLA Ops:
  0.6 36.5 %shard_map.77 = bf16[2,64,1024]{2,1,0:T(8,128)(2,1)S(1)} custom-call(bf16[128,512]{1,0:T(8,128)(2,1)} %ref_a.1, bf16[128,512]{1,0:T(8,128)(2,1)} %val_a.1, bf16[128,512]{1,0:T(8,128)(2,1)} %ref_b.1, bf16[128,512]{1,0:T(8,128)(2,1)} %val_b.1, bf16[512,1024]{1,0:T(8,128)(2,1)} %w_a.1, bf16[512,1024]{1,0:T(8,128)(2,1)} %w_b.1), custom_call_target="tpu_custom_call" | custom-call | tf_op jit(solution)/shard_map/pallas_call | solution.py:312
  37.1 0.7 %slice_bitcast_fusion = (bf16[64,1024]{1,0:T(8,128)(2,1)}, bf16[64,1024]{1,0:T(8,128)(2,1)}) fusion(bf16[2,64,1024]{2,1,0:T(8,128)(2,1)S(1)} %shard_map.77), kind=kLoop, calls=%fused_computation | loop fusion | bytes 524288 | tf_op jit(solution)/shard_map/squeeze | solution.py:349
